TPU v7x, 32 devices: a whole 2x2x4 slice. The times are simulated.
32 devices in a mesh: row: 8 (over z, y), col: 4 (over x, core).
Axes of the slice: x: 2, y: 2, z: 4, core: 2. Of those that a mesh axis runs over, the one named last changes fastest.
Arguments:
- window: float32 [2048, 8192], P('row', 'col'), may hold values from -6 to 6
- leaf_y: float32 [2, 2048, 256], P(None, 'row', 'col'), may hold values from -6 to 6
- tree_y: float32 [2, 3, 2048, 256], P(None, None, 'row', 'col'), may hold values from -6 to 6
Outputs:
- updated: float32 [2048, 8192], P('row', 'col')
All inputs are finite; a program needn't handle non-finite values.
Results may differ from a plain program's by a relative error of at most 0.0003.
Values sent between devices are 32-bit elements; how exact they have to be, the bound alone decides.
No kernel may reach another device: no remote copies, remote signals or barrier semaphores. Data moves between devices by JAX's collectives and lax.ppermute only.
A program may use at most 128 MiB of HBM per device.

v0:
```python
import jax
import jax.numpy as jnp
from jax import lax
from jax.sharding import PartitionSpec as P


def swapped(value, axis, apart):
    mask = 2**apart
    pairs = [(source, source ^ mask) for source in range(lax.axis_size(axis))]
    return lax.ppermute(value, axis, pairs)


def product(left, right):
    return jnp.dot(left, right, precision=lax.Precision.HIGHEST, preferred_element_type=jnp.float32)


def block_inverse(lower_block):
    width = lower_block.shape[0]
    diagonal = jnp.diagonal(lower_block)
    scaled = jnp.tril(lower_block, -1) / diagonal[:, None]
    power = -scaled
    inverse = jnp.eye(width, dtype=jnp.float32) + power
    reach = 2
    while reach < width:
        power = product(power, power)
        inverse = inverse + product(inverse, power)
        reach = reach * 2
    return inverse / diagonal[None, :]


def lower_inverse(gramian):
    width = gramian.shape[0]
    lower = jnp.tril(gramian.T, -1) + jnp.diag(jnp.diagonal(gramian)) * 0.5
    step = min(width, 32)
    identity = jnp.eye(width, dtype=jnp.float32)
    rows_done = []
    for start in range(0, width, step):
        right = identity[start : start + step]
        if start > 0:
            right = right - product(
                lower[start : start + step, :start], jnp.concatenate(rows_done, 0)
            )
        rows_done.append(
            product(block_inverse(lower[start : start + step, start : start + step]), right)
        )
    return jnp.concatenate(rows_done, 0)


def coefficients_of(gramian, inners):
    return product(lower_inverse(gramian), inners)


def per_device(window, leaf_y, tree_y):
    levels = lax.axis_size("row").bit_length() - 1
    panel_width = tree_y.shape[2]
    top_rows = window
    rest_rows = window[panel_width:]
    for panel_index in range(2):
        leaves = lax.all_gather(leaf_y[panel_index], "col", axis=1, tiled=True)
        trees = lax.all_gather(tree_y[panel_index], "col", axis=2, tiled=True)
        leaves_rest = leaves[panel_width:]
        leaf_gramian = product(leaves.T, leaves)
        leaf_inner = product(leaves.T, top_rows) + product(leaves_rest.T, rest_rows)
        leaf_coeff = coefficients_of(leaf_gramian, leaf_inner)
        top_rows = top_rows - product(leaves, leaf_coeff)
        rest_rows = rest_rows - product(leaves_rest, leaf_coeff)
        for level_index in range(levels):
            vectors = trees[level_index]
            gramian = product(vectors.T, vectors)
            inners = product(vectors.T, top_rows)
            far_inner, far_gramian = swapped((inners, gramian), "row", level_index)
            tree_coeff = coefficients_of(gramian + far_gramian, inners + far_inner)
            top_rows = top_rows - product(vectors, tree_coeff)
    return jnp.concatenate([top_rows, rest_rows], 0)


def solution(mesh):
    return jax.shard_map(
        per_device,
        mesh=mesh,
        in_specs=(P("row", "col"), P(None, "row", "col"), P(None, None, "row", "col")),
        out_specs=P("row", "col"),
        check_vma=False,
    )
```

profile of v0, /device:TPU:0, one launch (start us, length us, event | category | flops | bytes accessed | tf_op | source)
XLA Modules:
  0.0 859.3 jit_solution(10065386602275793163)
XLA Ops:
  1.1 10.0 %all-gather.3 = f32[1,3,256,256]{2,3,1,0:T(8,128)S(1)} all-gather(f32[1,3,256,64]{2,3,1,0:T(8,128)S(1)} %get-tuple-element.5), channel_id=5, replica_groups=mesh['row'=8,'col'=4] {'col'}, dimensions={3}, use_global_device_ids=true | all-gather | bytes 983040 | tf_op jit(solution)/shard_map/all_gather | solution.py:60
  11.5 2.7 collective-permute-start.10
  18.2 8.2 all-gather.1
  30.2 5.8 all-gather.2
  35.9 5.8 all-gather
  42.7 2.4 gather_fusion
  45.0 2.4 gather_fusion.36
  47.4 2.9 copy.6
  51.9 4.9 fusion.98
  57.7 2.4 gather_fusion.63
  61.1 2.4 gather_fusion.45
  64.5 2.4 gather_fusion.54
  67.9 2.5 gather_fusion.27
  72.3 2.6 gather_fusion.9
  76.6 2.6 gather_fusion.18
  79.2 2.6 fusion.84
  423.2 1.9 fusion.423
  425.2 3.6 fusion.7
  429.1 1.9 convolution_bitcast_fusion.12
  439.4 39.2 %collective-permute-done.1 = f32[256,2048]{0,1:T(8,128)S(1)} collective-permute-done((f32[256,2048]{0,1:T(8,128)S(1)}, f32[256,2048]{0,1:T(8,128)S(1)}, u32[]{:S(2)}, u32[]{:S(2)}) %collective-permute-start.1) | collective-permute-done | bytes 2097184 | tf_op jit(solution)/shard_map/ppermute | solution.py:10
  478.7 1.9 fusion.18
  480.6 3.6 fusion.6
  484.2 1.9 convolution_bitcast_fusion.10
  489.6 43.4 %collective-permute-done.3 = f32[256,2048]{0,1:T(8,128)S(1)} collective-permute-done((f32[256,2048]{0,1:T(8,128)S(1)}, f32[256,2048]{0,1:T(8,128)S(1)}, u32[]{:S(2)}, u32[]{:S(2)}) %collective-permute-start.3) | collective-permute-done | bytes 2097184 | tf_op jit(solution)/shard_map/ppermute | solution.py:10
  532.9 1.9 fusion.16
  534.8 4.0 fusion.5
  538.8 1.9 convolution_bitcast_fusion.8
  540.8 2.7 collective-permute-start.5
  545.3 87.2 %collective-permute-done.5 = f32[256,2048]{0,1:T(8,128)S(1)} collective-permute-done((f32[256,2048]{0,1:T(8,128)S(1)}, f32[256,2048]{0,1:T(8,128)S(1)}, u32[]{:S(2)}, u32[]{:S(2)}) %collective-permute-start.5) | collective-permute-done | bytes 2097184 | tf_op jit(solution)/shard_map/ppermute | solution.py:10
  632.5 1.9 fusion.14
  634.4 3.6 fusion.4
  638.0 1.9 fusion.89
  640.0 2.1 fusion.520
  642.1 3.6 fusion.3
  645.7 1.9 convolution_bitcast_fusion.5
  651.0 43.2 %collective-permute-done.7 = f32[256,2048]{0,1:T(8,128)S(1)} collective-permute-done((f32[256,2048]{0,1:T(8,128)S(1)}, f32[256,2048]{0,1:T(8,128)S(1)}, u32[]{:S(2)}, u32[]{:S(2)}) %collective-permute-start.7) | collective-permute-done | bytes 2097184 | tf_op jit(solution)/shard_map/ppermute | solution.py:10
  694.2 1.9 fusion.12
  696.1 3.8 fusion.2
  699.9 1.9 convolution_bitcast_fusion.3
  705.5 43.2 %collective-permute-done.9 = f32[256,2048]{0,1:T(8,128)S(1)} collective-permute-done((f32[256,2048]{0,1:T(8,128)S(1)}, f32[256,2048]{0,1:T(8,128)S(1)}, u32[]{:S(2)}, u32[]{:S(2)}) %collective-permute-start.9) | collective-permute-done | bytes 2097184 | tf_op jit(solution)/shard_map/ppermute | solution.py:10
  748.6 1.9 fusion.10
  750.5 3.6 fusion.1
  754.1 1.9 convolution_bitcast_fusion.1
  756.1 3.5 collective-permute-start.11
  761.4 87.5 %collective-permute-done.11 = f32[256,2048]{0,1:T(8,128)S(1)} collective-permute-done((f32[256,2048]{0,1:T(8,128)S(1)}, f32[256,2048]{0,1:T(8,128)S(1)}, u32[]{:S(2)}, u32[]{:S(2)}) %collective-permute-start.11) | collective-permute-done | bytes 2097184 | tf_op jit(solution)/shard_map/ppermute | solution.py:10
  848.8 2.2 fusion.8
  851.0 5.0 fusion
  856.0 2.9 copy.7
  (1173 shorter events, 377.9 us)
Async XLA Ops:
  11.5 39.9 %collective-permute-start.10 = (f32[256,256]{0,1:T(8,128)S(1)}, f32[256,256]{0,1:T(8,128)}, u32[]{:S(2)}, u32[]{:S(2)}) collective-permute-start(f32[256,256]{0,1:T(8,128)S(1)} %fusion.108), channel_id=1, source_target_pairs={{0,16},{4,20},{8,24},{12,28},{16,0},{20,4},{24,8},{28,12},{1,17},{... | collective-permute-start | bytes 786440 | tf_op jit(solution)/shard_map/ppermute | solution.py:10
  14.6 45.5 %collective-permute-start.6 = (f32[256,256]{0,1:T(8,128)S(1)}, f32[256,256]{0,1:T(8,128)}, u32[]{:S(2)}, u32[]{:S(2)}) collective-permute-start(f32[256,256]{0,1:T(8,128)S(1)} %fusion.106), channel_id=1, source_target_pairs={{0,4},{4,0},{8,12},{12,8},{16,20},{20,16},{24,28},{28,24},{1,5},{5... | collective-permute-start | bytes 786440 | tf_op jit(solution)/shard_map/ppermute | solution.py:10
  16.6 46.9 %collective-permute-start.8 = (f32[256,256]{0,1:T(8,128)S(1)}, f32[256,256]{0,1:T(8,128)}, u32[]{:S(2)}, u32[]{:S(2)}) collective-permute-start(f32[256,256]{0,1:T(8,128)S(1)} %fusion.107), channel_id=1, source_target_pairs={{0,8},{4,12},{8,0},{12,4},{16,24},{20,28},{24,16},{28,20},{1,9},{5... | collective-permute-start | bytes 786440 | tf_op jit(solution)/shard_map/ppermute | solution.py:10
  27.6 39.3 %collective-permute-start.4 = (f32[256,256]{0,1:T(8,128)}, f32[256,256]{0,1:T(8,128)}, u32[]{:S(2)}, u32[]{:S(2)}) collective-permute-start(f32[256,256]{0,1:T(8,128)} %fusion.105), channel_id=1, source_target_pairs={{0,16},{4,20},{8,24},{12,28},{16,0},{20,4},{24,8},{28,12},{1,17},{... | collective-permute-start | bytes 786440 | tf_op jit(solution)/shard_map/ppermute | solution.py:10
  29.0 41.4 %collective-permute-start = (f32[256,256]{0,1:T(8,128)}, f32[256,256]{0,1:T(8,128)}, u32[]{:S(2)}, u32[]{:S(2)}) collective-permute-start(f32[256,256]{0,1:T(8,128)} %fusion.103), channel_id=1, source_target_pairs={{0,4},{4,0},{8,12},{12,8},{16,20},{20,16},{24,28},{28,24},{1,5},{5... | collective-permute-start | bytes 786440 | tf_op jit(solution)/shard_map/ppermute | solution.py:10
  51.4 23.4 %collective-permute-start.2 = (f32[256,256]{0,1:T(8,128)}, f32[256,256]{0,1:T(8,128)}, u32[]{:S(2)}, u32[]{:S(2)}) collective-permute-start(f32[256,256]{0,1:T(8,128)} %fusion.104), channel_id=1, source_target_pairs={{0,8},{4,12},{8,0},{12,4},{16,24},{20,28},{24,16},{28,20},{1,9},{5... | collective-permute-start | bytes 786440 | tf_op jit(solution)/shard_map/ppermute | solution.py:10
  326.9 31.7 %copy-start.7 = (f32[256,256]{1,0:T(8,128)S(1)}, f32[256,256]{1,0:T(8,128)}, u32[]{:S(2)}) copy-start(f32[256,256]{1,0:T(8,128)} %copy-done.6) | copy-start | bytes 786436
  331.5 24.6 %copy-start.60 = (f32[32,32]{1,0:T(8,128)S(1)}, f32[32,32]{1,0:T(8,128)}, u32[]{:S(2)}) copy-start(f32[32,32]{1,0:T(8,128)} %fusion.578) | copy-start | bytes 12292
  331.5 24.8 %copy-start.95 = (f32[32,32]{1,0:T(8,128)S(1)}, f32[32,32]{1,0:T(8,128)}, u32[]{:S(2)}) copy-start(f32[32,32]{1,0:T(8,128)} %convolution_add_fusion.19) | copy-start | bytes 12292
  331.5 25.2 %copy-start.58 = (f32[32,32]{1,0:T(8,128)S(1)}, f32[32,32]{1,0:T(8,128)}, u32[]{:S(2)}) copy-start(f32[32,32]{1,0:T(8,128)} %fusion.581) | copy-start | bytes 12292
  331.5 25.4 %copy-start.94 = (f32[32,32]{1,0:T(8,128)S(1)}, f32[32,32]{1,0:T(8,128)}, u32[]{:S(2)}) copy-start(f32[32,32]{1,0:T(8,128)} %convolution_add_fusion.15) | copy-start | bytes 12292
  331.5 25.8 %copy-start.56 = (f32[32,32]{1,0:T(8,128)S(1)}, f32[32,32]{1,0:T(8,128)}, u32[]{:S(2)}) copy-start(f32[32,32]{1,0:T(8,128)} %fusion.584) | copy-start | bytes 12292
  331.5 26.0 %copy-start.93 = (f32[32,32]{1,0:T(8,128)S(1)}, f32[32,32]{1,0:T(8,128)}, u32[]{:S(2)}) copy-start(f32[32,32]{1,0:T(8,128)} %convolution_add_fusion.11) | copy-start | bytes 12292
  331.5 26.5 %copy-start.54 = (f32[32,32]{1,0:T(8,128)S(1)}, f32[32,32]{1,0:T(8,128)}, u32[]{:S(2)}) copy-start(f32[32,32]{1,0:T(8,128)} %fusion.587) | copy-start | bytes 12292
  331.5 26.6 %copy-start.92 = (f32[32,32]{1,0:T(8,128)S(1)}, f32[32,32]{1,0:T(8,128)}, u32[]{:S(2)}) copy-start(f32[32,32]{1,0:T(8,128)} %convolution_add_fusion.7) | copy-start | bytes 12292
  331.6 28.8 %copy-start.64 = (f32[32,32]{1,0:T(8,128)S(1)}, f32[32,32]{1,0:T(8,128)}, u32[]{:S(2)}) copy-start(f32[32,32]{1,0:T(8,128)} %fusion.517) | copy-start | bytes 12292
  331.6 28.9 %copy-start.96 = (f32[32,32]{1,0:T(8,128)S(1)}, f32[32,32]{1,0:T(8,128)}, u32[]{:S(2)}) copy-start(f32[32,32]{1,0:T(8,128)} %convolution_add_fusion.99) | copy-start | bytes 12292
  331.6 29.4 %copy-start.63 = (f32[32,32]{1,0:T(8,128)S(1)}, f32[32,32]{1,0:T(8,128)}, u32[]{:S(2)}) copy-start(f32[32,32]{1,0:T(8,128)} %fusion.514) | copy-start | bytes 12292
  331.6 30.8 %copy-start.62 = (f32[32,32]{1,0:T(8,128)S(1)}, f32[32,32]{1,0:T(8,128)}, u32[]{:S(2)}) copy-start(f32[32,32]{1,0:T(8,128)} %fusion.511) | copy-start | bytes 12292
  331.6 32.2 %copy-start.61 = (f32[32,32]{1,0:T(8,128)S(1)}, f32[32,32]{1,0:T(8,128)}, u32[]{:S(2)}) copy-start(f32[32,32]{1,0:T(8,128)} %fusion.508) | copy-start | bytes 12292
  331.6 33.6 %copy-start.59 = (f32[32,32]{1,0:T(8,128)S(1)}, f32[32,32]{1,0:T(8,128)}, u32[]{:S(2)}) copy-start(f32[32,32]{1,0:T(8,128)} %fusion.505) | copy-start | bytes 12292
  331.6 35.0 %copy-start.57 = (f32[32,32]{1,0:T(8,128)S(1)}, f32[32,32]{1,0:T(8,128)}, u32[]{:S(2)}) copy-start(f32[32,32]{1,0:T(8,128)} %fusion.502) | copy-start | bytes 12292
  333.8 34.1 %copy-start.55 = (f32[32,32]{1,0:T(8,128)S(1)}, f32[32,32]{1,0:T(8,128)}, u32[]{:S(2)}) copy-start(f32[32,32]{1,0:T(8,128)} %fusion.499) | copy-start | bytes 12292
  336.0 33.3 %copy-start.52 = (f32[32,32]{1,0:T(8,128)S(1)}, f32[32,32]{1,0:T(8,128)}, u32[]{:S(2)}) copy-start(f32[32,32]{1,0:T(8,128)} %fusion.496) | copy-start | bytes 12292
  338.2 32.5 %copy-start.50 = (f32[32,32]{1,0:T(8,128)S(1)}, f32[32,32]{1,0:T(8,128)}, u32[]{:S(2)}) copy-start(f32[32,32]{1,0:T(8,128)} %fusion.521) | copy-start | bytes 12292
  340.4 31.0 %copy-start.48 = (f32[32,32]{1,0:T(8,128)S(1)}, f32[32,32]{1,0:T(8,128)}, u32[]{:S(2)}) copy-start(f32[32,32]{1,0:T(8,128)} %fusion.524) | copy-start | bytes 12292
  342.6 29.4 %copy-start.46 = (f32[32,32]{1,0:T(8,128)S(1)}, f32[32,32]{1,0:T(8,128)}, u32[]{:S(2)}) copy-start(f32[32,32]{1,0:T(8,128)} %fusion.527) | copy-start | bytes 12292
  345.2 27.4 %copy-start.44 = (f32[32,32]{1,0:T(8,128)S(1)}, f32[32,32]{1,0:T(8,128)}, u32[]{:S(2)}) copy-start(f32[32,32]{1,0:T(8,128)} %fusion.530) | copy-start | bytes 12292
  347.4 25.9 %copy-start.42 = (f32[32,32]{1,0:T(8,128)S(1)}, f32[32,32]{1,0:T(8,128)}, u32[]{:S(2)}) copy-start(f32[32,32]{1,0:T(8,128)} %fusion.533) | copy-start | bytes 12292
  349.5 24.3 %copy-start.40 = (f32[32,32]{1,0:T(8,128)S(1)}, f32[32,32]{1,0:T(8,128)}, u32[]{:S(2)}) copy-start(f32[32,32]{1,0:T(8,128)} %fusion.536) | copy-start | bytes 12292
  366.4 23.3 %copy-start.30 = (f32[32,32]{1,0:T(8,128)S(1)}, f32[32,32]{1,0:T(8,128)}, u32[]{:S(2)}) copy-start(f32[32,32]{1,0:T(8,128)} %fusion.478) | copy-start | bytes 12292
  367.8 23.3 %copy-start.28 = (f32[32,32]{1,0:T(8,128)S(1)}, f32[32,32]{1,0:T(8,128)}, u32[]{:S(2)}) copy-start(f32[32,32]{1,0:T(8,128)} %fusion.481) | copy-start | bytes 12292
  369.2 23.3 %copy-start.26 = (f32[32,32]{1,0:T(8,128)S(1)}, f32[32,32]{1,0:T(8,128)}, u32[]{:S(2)}) copy-start(f32[32,32]{1,0:T(8,128)} %fusion.484) | copy-start | bytes 12292
  370.6 23.3 %copy-start.24 = (f32[32,32]{1,0:T(8,128)S(1)}, f32[32,32]{1,0:T(8,128)}, u32[]{:S(2)}) copy-start(f32[32,32]{1,0:T(8,128)} %fusion.487) | copy-start | bytes 12292
  371.8 23.3 %copy-start.20 = (f32[32,32]{1,0:T(8,128)S(1)}, f32[32,32]{1,0:T(8,128)}, u32[]{:S(2)}) copy-start(f32[32,32]{1,0:T(8,128)} %fusion.493) | copy-start | bytes 12292
  372.4 23.3 %copy-start.39 = (f32[32,32]{1,0:T(8,128)S(1)}, f32[32,32]{1,0:T(8,128)}, u32[]{:S(2)}) copy-start(f32[32,32]{1,0:T(8,128)} %fusion.420) | copy-start | bytes 12292
  373.0 24.1 %copy-start.36 = (f32[32,32]{1,0:T(8,128)S(1)}, f32[32,32]{1,0:T(8,128)}, u32[]{:S(2)}) copy-start(f32[32,32]{1,0:T(8,128)} %fusion.417) | copy-start | bytes 12292
  373.7 24.1 %copy-start.33 = (f32[32,32]{1,0:T(8,128)S(1)}, f32[32,32]{1,0:T(8,128)}, u32[]{:S(2)}) copy-start(f32[32,32]{1,0:T(8,128)} %fusion.414) | copy-start | bytes 12292
  374.3 24.1 %copy-start.31 = (f32[32,32]{1,0:T(8,128)S(1)}, f32[32,32]{1,0:T(8,128)}, u32[]{:S(2)}) copy-start(f32[32,32]{1,0:T(8,128)} %fusion.411) | copy-start | bytes 12292
  374.9 24.1 %copy-start.29 = (f32[32,32]{1,0:T(8,128)S(1)}, f32[32,32]{1,0:T(8,128)}, u32[]{:S(2)}) copy-start(f32[32,32]{1,0:T(8,128)} %fusion.408) | copy-start | bytes 12292
  375.5 24.1 %copy-start.27 = (f32[32,32]{1,0:T(8,128)S(1)}, f32[32,32]{1,0:T(8,128)}, u32[]{:S(2)}) copy-start(f32[32,32]{1,0:T(8,128)} %fusion.405) | copy-start | bytes 12292
  376.9 23.3 %copy-start.25 = (f32[32,32]{1,0:T(8,128)S(1)}, f32[32,32]{1,0:T(8,128)}, u32[]{:S(2)}) copy-start(f32[32,32]{1,0:T(8,128)} %fusion.402) | copy-start | bytes 12292
  431.0 47.7 %collective-permute-start.1 = (f32[256,2048]{0,1:T(8,128)S(1)}, f32[256,2048]{0,1:T(8,128)S(1)}, u32[]{:S(2)}, u32[]{:S(2)}) collective-permute-start(f32[256,2048]{0,1:T(8,128)S(1)} %convolution_bitcast_fusion.12), channel_id=1, source_target_pairs={{0,4},{4,0},{8,12},{12,8},{16,20},{20,16},{24,28},{28,24},{1,5},{5... | collective-permute-start | bytes 6291464 | tf_op jit(solution)/shard_map/ppermute | solution.py:10
  486.1 46.8 %collective-permute-start.3 = (f32[256,2048]{0,1:T(8,128)S(1)}, f32[256,2048]{0,1:T(8,128)S(1)}, u32[]{:S(2)}, u32[]{:S(2)}) collective-permute-start(f32[256,2048]{0,1:T(8,128)S(1)} %convolution_bitcast_fusion.10), channel_id=1, source_target_pairs={{0,8},{4,12},{8,0},{12,4},{16,24},{20,28},{24,16},{28,20},{1,9},{5... | collective-permute-start | bytes 6291464 | tf_op jit(solution)/shard_map/ppermute | solution.py:10
  540.8 91.7 %collective-permute-start.5 = (f32[256,2048]{0,1:T(8,128)S(1)}, f32[256,2048]{0,1:T(8,128)S(1)}, u32[]{:S(2)}, u32[]{:S(2)}) collective-permute-start(f32[256,2048]{0,1:T(8,128)S(1)} %convolution_bitcast_fusion.8), channel_id=1, source_target_pairs={{0,16},{4,20},{8,24},{12,28},{16,0},{20,4},{24,8},{28,12},{1,17},{... | collective-permute-start | bytes 6291464 | tf_op jit(solution)/shard_map/ppermute | solution.py:10
  647.7 46.5 %collective-permute-start.7 = (f32[256,2048]{0,1:T(8,128)S(1)}, f32[256,2048]{0,1:T(8,128)S(1)}, u32[]{:S(2)}, u32[]{:S(2)}) collective-permute-start(f32[256,2048]{0,1:T(8,128)S(1)} %convolution_bitcast_fusion.5), channel_id=1, source_target_pairs={{0,4},{4,0},{8,12},{12,8},{16,20},{20,16},{24,28},{28,24},{1,5},{5... | collective-permute-start | bytes 6291464 | tf_op jit(solution)/shard_map/ppermute | solution.py:10
  701.8 46.8 %collective-permute-start.9 = (f32[256,2048]{0,1:T(8,128)S(1)}, f32[256,2048]{0,1:T(8,128)S(1)}, u32[]{:S(2)}, u32[]{:S(2)}) collective-permute-start(f32[256,2048]{0,1:T(8,128)S(1)} %convolution_bitcast_fusion.3), channel_id=1, source_target_pairs={{0,8},{4,12},{8,0},{12,4},{16,24},{20,28},{24,16},{28,20},{1,9},{5... | collective-permute-start | bytes 6291464 | tf_op jit(solution)/shard_map/ppermute | solution.py:10
  756.1 92.7 %collective-permute-start.11 = (f32[256,2048]{0,1:T(8,128)S(1)}, f32[256,2048]{0,1:T(8,128)S(1)}, u32[]{:S(2)}, u32[]{:S(2)}) collective-permute-start(f32[256,2048]{0,1:T(8,128)S(1)} %convolution_bitcast_fusion.1), channel_id=1, source_target_pairs={{0,16},{4,20},{8,24},{12,28},{16,0},{20,4},{24,8},{28,12},{1,17},{... | collective-permute-start | bytes 6291464 | tf_op jit(solution)/shard_map/ppermute | solution.py:10
  (182 other events, 2309.5 us)
where the time goes:
time: 875 us; the launch traced here: 859 us
  matrix products  373 us (43%)
  waiting for transfers between devices  344 us (39%)
  local copies, waits for them, and re-layouts  75.9 us (9%)
  blocking collectives  29.9 us (3%)
  starting transfers between devices  19.9 us (2%)
  other arithmetic  10.7 us (1%)
    dot_general x664, matrix products, product(): jnp.dot(left, right, precision=lax.Precision.HIGHEST, preferred_element_t...  373 us
    ppermute x12, waiting for transfers between devices, swapped(): return lax.ppermute(value, axis, pairs)  344 us
    gather x64, local copies, waits for them, and re-layouts, block_inverse(): diagonal = jnp.diagonal(lower_block)  46.3 us
    ppermute x12, starting transfers between devices, swapped(): return lax.ppermute(value, axis, pairs)  19.9 us
    gather x8, local copies, waits for them, and re-layouts, lower_inverse(): lower = jnp.tril(gramian.T, -1) + jnp.diag(jnp.diagonal(gramian)) * 0.5  19.6 us
    all_gather x2, blocking collectives, per_device(): trees = lax.all_gather(tree_y[panel_index], 'col', axis=2, tiled=True)  18.2 us
  transfers between devices with their start and end apart: 12, of which 6 were waited for; matrix products, arithmetic and copies ran while one was open for 6% of the time, Pallas kernels for 0%

commit v1 on v0

v1 whole, which is shorter than its diff:
```python
import functools

import jax
import jax.numpy as jnp
from jax import lax
from jax.experimental import pallas as pl
from jax.experimental.pallas import tpu as pltpu
from jax.sharding import PartitionSpec as P

F32, BF16 = jnp.float32, jnp.bfloat16
NN, NT = ((1,), (0,)), ((1,), (1,))
CHUNKS = 2
VMEM_BYTES = 50 * 2**20


def halves(value):
    high = value.astype(BF16)
    return high, (value - high.astype(F32)).astype(BF16)


def dot(left, right, dims):
    return lax.dot_general(left, right, (dims, ((), ())), preferred_element_type=F32)


def multiply(left, right, dims=NN):
    (left_high, left_low), (right_high, right_low) = left, right
    return dot(left_high, right_high, dims) + (
        dot(left_high, right_low, dims) + dot(left_low, right_high, dims)
    )


def iotas(rows, columns):
    shape = (rows, columns)
    return lax.broadcasted_iota(jnp.int32, shape, 0), lax.broadcasted_iota(jnp.int32, shape, 1)


def spread(compact, mask):
    times = mask.shape[0] // compact.shape[0]
    full = compact if times == 1 else jnp.concatenate([compact] * times, 0)
    return jnp.where(mask, full, 0.0)


def triangle_inverses(gramians):
    width = gramians[0].shape[0]
    size = min(width, 32)
    row, column = iotas(width, width)
    scaled = []
    for gramian in gramians:
        diagonal = jnp.where(row == column, gramian, 0.0)
        across = 1.0 / jnp.sqrt(0.5 * jnp.sum(diagonal, 0, keepdims=True))
        down = 1.0 / jnp.sqrt(0.5 * jnp.sum(diagonal, 1, keepdims=True))
        scaled.append((jnp.where(row < column, gramian * down * across, 0.0), across, down))
    small_row, small_column = iotas(size, width)
    unit = jnp.where(small_row == small_column % size, 1.0, 0.0)
    mask = row // size == column // size
    inverses = []
    stacks = []
    for upper, _, _ in scaled:
        block = jnp.where(mask, -upper, 0.0)
        compact = block[:size]
        for start in range(size, width, size):
            compact = compact + block[start : start + size]
        stacks.append((unit + compact, multiply(halves(compact), halves(block))))
    reach = 2
    while reach < size:
        last = reach * 2 >= size
        following = []
        for inverse, power in stacks:
            left = inverse if last else jnp.concatenate([inverse, power], 0)
            both = multiply(halves(left), halves(spread(power, mask)))
            following.append((inverse + both[:size], None if last else both[size:]))
        stacks = following
        reach *= 2
    inverses = [inverse for inverse, _ in stacks]
    while size < width:
        small_row, small_column = iotas(size, width)
        even = (small_column // size) % 2 == 0
        block_row, block_column = row // size, column // size
        mask = block_row == block_column
        beside = (block_row % 2 == 0) & (block_column == block_row + 1)
        following = []
        for inverse, (upper, _, _) in zip(inverses, scaled):
            top = jnp.where(even, inverse, 0.0)
            step = multiply(halves(top), halves(jnp.where(beside, upper, 0.0)))
            step = multiply(halves(step), halves(spread(inverse, mask)))
            following.append(jnp.concatenate([top - step, inverse - top], 0))
        inverses = following
        size *= 2
    return [(inverse, across, down) for inverse, (_, across, down) in zip(inverses, scaled)]


def reflectors_of(vectors_t, inverse):
    solved, across, down = inverse
    return multiply(halves((vectors_t * down).T), halves(solved), NT) * across


def store(high_ref, low_ref, index, value):
    high_ref[index], low_ref[index] = halves(value)


def operator(high_ref, low_ref, *index):
    return (high_ref[index], low_ref[index]) if index else (high_ref[...], low_ref[...])


def assemble(position, near_ref, far_ref, columns, group, block, into, index):
    half = len(columns) // 2
    width = near_ref.shape[-2]
    for at, offset in enumerate(columns):
        ref = near_ref if at < half else far_ref
        where = pl.multiple_of((position ^ offset) * width, width)
        into[(*index, pl.ds(where, width), slice(None))] = ref[at % half, group, block]


def home_gramians(columns, low, position_ref, near_ref, far_ref, vectors_ref, send_ref):
    position = position_ref[0]
    shard = near_ref.shape[-2]
    for block in range(vectors_ref.shape[0]):
        assemble(position, near_ref, far_ref, columns, 0, block, vectors_ref, (block,))
    width = vectors_ref.shape[1]
    for level in range(low):
        first, second = halves(vectors_ref[1 + level]), halves(vectors_ref[1 + low + level])
        send_ref[level, :width] = multiply(first, first, NT)
        own = vectors_ref[1 + low + level, pl.ds(pl.multiple_of(position * shard, shard), shard), :]
        send_ref[level, width:] = multiply(halves(own), second, NT)


def home_leaf(has_next, vectors_ref, high_ref, low_ref):
    vectors_t = vectors_ref[0]
    pair = halves(vectors_t)
    (inverse,) = triangle_inverses([multiply(pair, pair, NT)])
    width = vectors_t.shape[1]
    row, column = iotas(width, width)
    step = multiply(halves(reflectors_of(vectors_t, inverse)), pair)
    leaf = jnp.where(row == column, 1.0, 0.0) - step
    rows = leaf.shape[0]
    high_ref[:rows], low_ref[:rows] = halves(leaf)
    if has_next:
        high_ref[rows:], low_ref[rows:] = halves(multiply(halves(vectors_ref[1]), halves(leaf)))


def home_tree(low, vectors_ref, own_ref, far_ref, high_ref, low_ref):
    width = vectors_ref.shape[1]
    sums = [own_ref[level, :width] + far_ref[level, :width] for level in range(low)]
    for level, inverse in enumerate(triangle_inverses(sums)):
        store(high_ref, low_ref, level, reflectors_of(vectors_ref[1 + level], inverse))


def top_tree(columns, places, blocks, position_ref, near_ref, far_ref, *refs):
    yt_high, yt_low, v_high, v_low, vectors = refs
    position = position_ref[0]
    groups, levels = len(places), len(blocks)
    sums = []
    for level, block in enumerate(blocks):
        apart = 2**level
        gramians = []
        for group in range(groups):
            assemble(position, near_ref, far_ref, columns, places[group], block, vectors, (level, group))
            pair = halves(vectors[level, group])
            yt_high[level, group], yt_low[level, group] = pair
            gramians.append(multiply(pair, pair, NT))
        sums += [gramians[g] + gramians[g ^ apart] for g in range(groups) if g < g ^ apart]
    inverses = iter(triangle_inverses(sums))
    for level in range(levels):
        apart = 2**level
        for group in range(groups):
            if group < group ^ apart:
                inverse = next(inverses)
                for member in (group, group ^ apart):
                    store(v_high, v_low, (level, member), reflectors_of(vectors[level, member], inverse))


def top_leaf(columns, places, low, position_ref, near_ref, far_ref, *refs):
    a_high, a_low, yt_high, yt_low, vectors = refs
    position = position_ref[0]
    width = vectors.shape[-1]
    gramians = []
    for group, where in enumerate(places):
        assemble(position, near_ref, far_ref, columns, where, 0, vectors, (group, 0))
        pair = halves(vectors[group, 0])
        gramians.append(multiply(pair, pair, NT))
        for level in range(low):
            assemble(position, near_ref, far_ref, columns, where, 1 + level, vectors, (group, 1))
            store(yt_high, yt_low, (level, group), vectors[group, 1])
    row, column = iotas(vectors.shape[-1], vectors.shape[-1])
    for group, inverse in enumerate(triangle_inverses(gramians)):
        vectors_t = vectors[group, 0]
        step = multiply(halves(reflectors_of(vectors_t, inverse)), halves(vectors_t))
        store(a_high, a_low, group, jnp.where(row == column, 1.0, 0.0) - step)


def top_low(columns, places, low, position_ref, near_ref, far_ref, gram_near, gram_far, *refs):
    v_high, v_low, vectors, gramians = refs
    position = position_ref[0]
    for level in range(low):
        for group, where in enumerate(places):
            assemble(position, near_ref, far_ref, columns, where, 1 + level, vectors, (group,))
            assemble(position, gram_near, gram_far, columns, where, level, gramians, (group,))
        inverses = triangle_inverses([gramians[group] for group in range(len(places))])
        for group, inverse in enumerate(inverses):
            store(v_high, v_low, (level, group), reflectors_of(vectors[group], inverse))


def home_start(window_ref, high_ref, low_ref, out_ref, *inner_ref):
    both = multiply(operator(high_ref, low_ref), halves(window_ref[...]))
    rows = out_ref.shape[0]
    out_ref[...] = both[:rows]
    if inner_ref:
        inner_ref[0][...] = both[rows:]


def home_level(top_ref, own_ref, far_ref, v_high, v_low, yt_ref, out_ref, inner_ref):
    inner = own_ref[...] + far_ref[...]
    out = top_ref[...] - multiply(operator(v_high, v_low), halves(inner))
    out_ref[...] = out
    inner_ref[...] = multiply(halves(yt_ref[...]), halves(out))


def home_last(groups, position_ref, top_ref, own_ref, far_ref, v_high, v_low, *out_refs):
    width = top_ref.shape[1] // groups
    pair = operator(v_high, v_low)
    for group, out_ref in enumerate(out_refs):
        at = pl.ds(pl.multiple_of((position_ref[0] ^ group) * width, width), width)
        inner = own_ref[:, at] + far_ref[:, at]
        out_ref[...] = top_ref[:, at] - multiply(pair, halves(inner))


def top_levels(tops, levels, yt_high, yt_low, v_high, v_low):
    groups = len(tops)
    for level in range(levels):
        apart = 2**level
        inners = [multiply(operator(yt_high, yt_low, level, g), halves(tops[g])) for g in range(groups)]
        sums = [halves(inners[g] + inners[g ^ apart]) for g in range(groups) if g < g ^ apart]
        order = [g for g in range(groups) if g < g ^ apart]
        tops = [
            tops[g] - multiply(operator(v_high, v_low, level, g), sums[order.index(min(g, g ^ apart))])
            for g in range(groups)
        ]
    return tops


def middle(groups, levels, low, *refs):
    pieces, refs = refs[:groups], refs[groups:]
    yt_high, yt_low, v_high, v_low, a_high, a_low, e_high, e_low = refs[:8]
    out_ref = refs[8]
    tops = top_levels([ref[...] for ref in pieces], levels, yt_high, yt_low, v_high, v_low)
    for g in range(groups):
        top = multiply(operator(a_high, a_low, g), halves(tops[g]))
        out_ref[g] = top
        if low:
            refs[9][g] = multiply(operator(e_high, e_low, 0, g), halves(top))


def low_step(groups, level, top_ref, own_ref, far_ref, v_high, v_low, yt_high, yt_low, out_ref, inner_ref):
    for g in range(groups):
        inner = own_ref[g] + far_ref[g]
        top = top_ref[g] - multiply(operator(v_high, v_low, level, g), halves(inner))
        out_ref[g] = top
        inner_ref[g] = multiply(operator(yt_high, yt_low, level + 1, g), halves(top))


def finish(groups, levels, low, *refs):
    top_ref, refs = refs[0], refs[1:]
    tops = [top_ref[g] for g in range(groups)]
    if low:
        own_ref, far_ref, b_high, b_low = refs[:4]
        refs = refs[4:]
        tops = [
            tops[g] - multiply(operator(b_high, b_low, low - 1, g), halves(own_ref[g] + far_ref[g]))
            for g in range(groups)
        ]
    tops = top_levels(tops, levels, *refs[:4])
    for g, out_ref in enumerate(refs[4:]):
        out_ref[...] = tops[g]


def place(groups, chunks, position_ref, *refs):
    out_ref = refs[-1]
    width = refs[0].shape[1]
    for chunk in range(chunks):
        for g in range(groups):
            at = (chunk * groups + (position_ref[0] ^ g)) * width
            out_ref[:, pl.ds(pl.multiple_of(at, width), width)] = refs[chunk * groups + g][...]


def call(kernel, outs, operands, flops, scalars=0, scratch=()):
    in_memory = pl.BlockSpec(memory_space=pltpu.VMEM)
    specs = [pl.BlockSpec(memory_space=pltpu.SMEM)] * scalars + [in_memory] * (len(operands) - scalars)
    shapes = [jax.ShapeDtypeStruct(*out) for out in outs]
    moved = sum(x.size * x.dtype.itemsize for x in [*operands, *shapes])
    result = pl.pallas_call(
        kernel,
        out_shape=shapes,
        in_specs=specs,
        out_specs=[in_memory] * len(shapes),
        scratch_shapes=[pltpu.VMEM(*s) for s in scratch],
        compiler_params=pltpu.CompilerParams(vmem_limit_bytes=VMEM_BYTES),
        cost_estimate=pl.CostEstimate(flops=int(flops), bytes_accessed=int(moved), transcendentals=0),
    )(*operands)
    return result


def swapped(value, axis, mask):
    pairs = [(source, source ^ mask) for source in range(lax.axis_size(axis))]
    return lax.ppermute(value, axis, pairs)


def per_device(window, leaf_y, tree_y):
    rows, across = window.shape
    width = tree_y.shape[2]
    levels = lax.axis_size("row").bit_length() - 1
    top = min(2, levels)
    low = levels - top
    groups = 2**top
    row_at, col_at = lax.axis_index("row"), lax.axis_index("col")
    column_at = jnp.reshape(col_at, (1,)).astype(jnp.int32)
    group_at = jnp.reshape(row_at // 2**low, (1,)).astype(jnp.int32)
    col_masks = [2**bit for bit in reversed(range(lax.axis_size("col").bit_length() - 1))]
    columns = [0]
    for mask in col_masks:
        columns = columns + [offset ^ mask for offset in columns]
    unit = 2 * width**3 * 3

    leaf_t, tree_t = jnp.swapaxes(leaf_y, 1, 2), jnp.swapaxes(tree_y, 2, 3)

    def over_col(value):
        for mask in col_masks[:-1]:
            value = jnp.concatenate([value, swapped(value, "col", mask)], 0)
        return value, swapped(value, "col", col_masks[-1])

    order = [0]
    for bit in reversed(range(top)):
        order = order + [offset ^ 2**bit for offset in order]
    places = [order.index(offset) for offset in range(groups)]

    home_shard = jnp.concatenate([leaf_t[:1], tree_t[0, :low], tree_t[1, :low]], 0)
    home_near, home_far = over_col(home_shard[None, None])

    def over_all(value):
        value = value[None]
        for bit in reversed(range(top)):
            value = jnp.concatenate([value, swapped(value, "row", 2 ** (low + bit))], 0)
        return over_col(value[None])

    first_near, first_far = over_all(tree_t[0, low:])
    second_near, second_far = over_all(jnp.concatenate([leaf_t[1:], tree_t[1]], 0))

    blocks = home_shard.shape[0]
    vectors, sends = call(
        functools.partial(home_gramians, columns, low),
        [((blocks, width, rows), F32), ((max(low, 1), width + home_shard.shape[1], width), F32)],
        [column_at, home_near, home_far],
        unit * 2 * max(low, 1),
        scalars=1,
    )
    a_high, a_low = call(
        functools.partial(home_leaf, low > 0),
        [((rows + (width if low else 0), rows), BF16)] * 2,
        [vectors],
        unit * 8,
    )
    if low:
        fars = jnp.stack([swapped(sends[level], "row", 2**level) for level in range(low)])
        v_high, v_low = call(
            functools.partial(home_tree, low),
            [((low, rows, width), BF16)] * 2,
            [vectors, sends, fars],
            unit * 6 * low,
        )
        gram_shard = sends[:, width:] + fars[:, width:]
        gram_near, gram_far = over_all(gram_shard)

    kept = [((top, groups, width, rows), BF16)] * 2 + [((top, groups, rows, width), BF16)] * 2
    scratch = [((top, groups, width, rows), F32)]
    first_ops = call(
        functools.partial(top_tree, columns, places, list(range(top))),
        kept,
        [column_at, first_near, first_far],
        unit * 28,
        scalars=1,
        scratch=scratch,
    )
    leaf_ops = call(
        functools.partial(top_leaf, columns, places, low),
        [((groups, rows, rows), BF16)] * 2 + [((max(low, 1), groups, width, rows), BF16)] * 2,
        [column_at, second_near, second_far],
        unit * 32,
        scalars=1,
        scratch=[((groups, 2, width, rows), F32)],
    )
    if low:
        low_ops = call(
            functools.partial(top_low, columns, places, low),
            [((low, groups, rows, width), BF16)] * 2,
            [column_at, second_near, second_far, gram_near, gram_far],
            unit * 20 * low,
            scalars=1,
            scratch=[((groups, width, rows), F32), ((groups, width, width), F32)],
        )
    second_ops = call(
        functools.partial(top_tree, columns, places, [1 + low + l for l in range(top)]),
        kept,
        [column_at, second_near, second_far],
        unit * 28,
        scalars=1,
        scratch=scratch,
    )

    chunks = max(1, min(CHUNKS, across // groups // 128))
    wide = across // chunks
    narrow = wide // groups
    work = unit * wide // width
    piece = ((rows, narrow), F32)
    stack = ((groups, rows, narrow), F32)
    whole = ((rows, wide), F32)
    inner = ((width, wide), F32)
    results = []
    for chunk in range(chunks):
        part = window[:, chunk * wide : (chunk + 1) * wide]
        if low:
            here, own = call(home_start, [whole, inner], [part, a_high, a_low], work * 2)
            for level in range(low):
                far = swapped(own, "row", 2**level)
                if level < low - 1:
                    here, own = call(
                        home_level,
                        [whole, inner],
                        [here, own, far, v_high[level], v_low[level], vectors[2 + level]],
                        work * 2,
                    )
            pieces = call(
                functools.partial(home_last, groups),
                [piece] * groups,
                [group_at, here, own, far, v_high[low - 1], v_low[low - 1]],
                work,
                scalars=1,
            )
        else:
            (here,) = call(home_start, [whole], [part, a_high, a_low], work)
            pieces = [
                lax.dynamic_slice_in_dim(here, (group_at[0] ^ g) * narrow, narrow, 1) for g in range(groups)
            ]
        pieces = [pieces[0]] + [swapped(pieces[g], "row", g << low) for g in range(1, groups)]
        if low:
            here, own = call(
                functools.partial(middle, groups, top, low),
                [stack, ((groups, width, narrow), F32)],
                [*pieces, *first_ops, *leaf_ops],
                work * 6,
            )
            for level in range(low):
                far = swapped(own, "row", 2**level)
                if level < low - 1:
                    here, own = call(
                        functools.partial(low_step, groups, level),
                        [stack, ((groups, width, narrow), F32)],
                        [here, own, far, *low_ops, *leaf_ops[2:]],
                        work * 2,
                    )
            operands = [here, own, far, *low_ops, *second_ops]
        else:
            (here,) = call(
                functools.partial(middle, groups, top, low), [stack], [*pieces, *first_ops, *leaf_ops], work * 5
            )
            operands = [here, *second_ops]
        pieces = call(functools.partial(finish, groups, top, low), [piece] * groups, operands, work * 5)
        results += [pieces[0]] + [swapped(pieces[g], "row", g << low) for g in range(1, groups)]
    (updated,) = call(
        functools.partial(place, groups, chunks), [((rows, across), F32)], [group_at, *results], 0, scalars=1
    )
    return updated


def solution(mesh):
    return jax.shard_map(
        per_device,
        mesh=mesh,
        in_specs=(P("row", "col"), P(None, "row", "col"), P(None, None, "row", "col")),
        out_specs=P("row", "col"),
        check_vma=False,
    )
```

time: 875 us -> 265 us (0.30); the launches traced: 859 us -> 260 us
  matrix products: 373 us -> 0 us
  waiting for transfers between devices: 344 us -> 111 us
  Pallas kernels: 0 us -> 70.5 us
  local copies, waits for them, and re-layouts: 75.9 us -> 13.7 us
  starting transfers between devices: 19.9 us -> 60.1 us
  blocking collectives: 29.9 us -> 0 us
    dot_general x664 -> x0, matrix products: 373 us -> none  [product(): jnp.dot(left, right, precision=lax.Precision.HIGHEST, preferred_element_t...]
    ppermute x12 -> x31, waiting for transfers between devices: 344 us -> 111 us  [swapped(): return lax.ppermute(value, axis, pairs)]
    pallas_call x0 -> x16, Pallas kernels: none -> 70.5 us  [call(): pl.pallas_call(kernel, out_shape=shapes, in_specs=specs, out_specs=[in_me...]
    gather x72 -> x0, local copies, waits for them, and re-layouts: 65.9 us -> none  [the longest x64 46.3 us: block_inverse(): diagonal = jnp.diagonal(lower_block)]
    ppermute x12 -> x31, starting transfers between devices: 19.9 us -> 60.1 us  [swapped(): return lax.ppermute(value, axis, pairs)]
    all_gather x4 -> x0, blocking collectives: 29.9 us -> none  [the longest x2 18.2 us: per_device(): trees = lax.all_gather(tree_y[panel_index], 'col', axis=2, tiled=True)]
    add x9 -> x0, other arithmetic: 10.7 us -> none  [the longest x6 7.57 us: per_device(): tree_coeff = coefficients_of(gramian + far_gramian, inners + far_inner)]
  transfers between devices with their start and end apart: 12 -> 31, of which waited for: 6 -> 12; matrix products, arithmetic and copies ran while one was open for 6% -> 2% of each run, Pallas kernels for 0% -> 27%
where the time goes in v1:
time: 265 us; the launch traced here: 260 us
  waiting for transfers between devices  111 us (42%)
  Pallas kernels  70.5 us (27%)
  starting transfers between devices  60.1 us (23%)
  local copies, waits for them, and re-layouts  13.7 us (5%)
  other arithmetic  4.42 us (2%)
    ppermute x31, waiting for transfers between devices, swapped(): return lax.ppermute(value, axis, pairs)  111 us
    pallas_call x16, Pallas kernels, call(): pl.pallas_call(kernel, out_shape=shapes, in_specs=specs, out_specs=[in_me...  70.5 us
    ppermute x31, starting transfers between devices, swapped(): return lax.ppermute(value, axis, pairs)  60.1 us
    unnamed x36, local copies, waits for them, and re-layouts  11.5 us
  transfers between devices with their start and end apart: 31, of which 12 were waited for; matrix products, arithmetic and copies ran while one was open for 2% of the time, Pallas kernels for 27%

profile of v1, /device:TPU:0, one launch (start us, length us, event | category | flops | bytes accessed | tf_op | source)
XLA Modules:
  0.0 260.3 jit_solution(4242657082934494023)
XLA Ops:
  1.9 4.1 %collective-permute-start.11 = (f32[1,4,64,256]{3,2,1,0:T(8,128)S(1)}, f32[1,4,64,256]{3,2,1,0:T(8,128)S(1)}, u32[]{:S(2)}, u32[]{:S(2)}) collective-permute-start(f32[1,4,64,256]{3,2,1,0:T(8,128)S(1)} %maximum_bitcast_fusion.2), channel_id=1, source_target_pairs={{0,16},{4,20},{8,24},{12,28},{16,0},{20,4},{24,8},{28,12},{1,17},{... | collective-permute-start | bytes 786440 | tf_op jit(solution)/shard_map/ppermute | solution.py:304
  6.0 11.9 %collective-permute-done.11 = f32[1,4,64,256]{3,2,1,0:T(8,128)S(1)} collective-permute-done((f32[1,4,64,256]{3,2,1,0:T(8,128)S(1)}, f32[1,4,64,256]{3,2,1,0:T(8,128)S(1)}, u32[]{:S(2)}, u32[]{:S(2)}) %collective-permute-start.11) | collective-permute-done | bytes 262176 | tf_op jit(solution)/shard_map/ppermute | solution.py:304
  18.8 12.4 %collective-permute-done.12 = f32[2,4,64,256]{3,2,1,0:T(8,128)S(1)} collective-permute-done((f32[2,4,64,256]{3,2,1,0:T(8,128)S(1)}, f32[2,4,64,256]{3,2,1,0:T(8,128)S(1)}, u32[]{:S(2)}, u32[]{:S(2)}) %collective-permute-start.12) | collective-permute-done | bytes 524320 | tf_op jit(solution)/shard_map/ppermute | solution.py:304
  31.3 1.3 collective-permute-start.13
  32.6 3.4 %collective-permute-start.7 = (f32[1,2,64,256]{3,2,1,0:T(8,128)S(1)}, f32[1,2,64,256]{3,2,1,0:T(8,128)S(1)}, u32[]{:S(2)}, u32[]{:S(2)}) collective-permute-start(f32[1,2,64,256]{3,2,1,0:T(8,128)S(1)} %slice.43), channel_id=1, source_target_pairs={{0,16},{4,20},{8,24},{12,28},{16,0},{20,4},{24,8},{28,12},{1,17},{... | collective-permute-start | bytes 393224 | tf_op jit(solution)/shard_map/ppermute | solution.py:304
  36.6 5.0 %collective-permute-done.7 = f32[1,2,64,256]{3,2,1,0:T(8,128)S(1)} collective-permute-done((f32[1,2,64,256]{3,2,1,0:T(8,128)S(1)}, f32[1,2,64,256]{3,2,1,0:T(8,128)S(1)}, u32[]{:S(2)}, u32[]{:S(2)}) %collective-permute-start.7) | collective-permute-done | bytes 131104 | tf_op jit(solution)/shard_map/ppermute | solution.py:304
  42.5 16.5 %collective-permute-done = f32[1,1,3,64,256]{4,3,2,1,0:T(8,128)S(1)} collective-permute-done((f32[1,1,3,64,256]{4,3,2,1,0:T(8,128)S(1)}, f32[1,1,3,64,256]{4,3,2,1,0:T(8,128)S(1)}, u32[]{:S(2)}, u32[]{:S(2)}) %collective-permute-start) | collective-permute-done | bytes 196640 | tf_op jit(solution)/shard_map/ppermute | solution.py:304
  59.1 1.5 pad_maximum_fusion.near_ref
  61.1 1.3 collective-permute-start.9
  63.2 1.6 collective-permute-start.3
  64.8 3.7 %shard_map.38 = (bf16[512,256]{1,0:T(8,128)(2,1)S(1)}, bf16[512,256]{1,0:T(8,128)(2,1)S(1)}) custom-call(f32[3,256,256]{2,1,0:T(8,128)S(1)} %get-tuple-element.49.vectors_ref), custom_call_target="tpu_custom_call" | custom-call | flops 805306368 | bytes 1310720 | tf_op jit(solution)/shard_map/pallas_call | solution.py:290
  68.5 2.0 shard_map.39
  72.0 1.6 collective-permute-start.23
  73.6 1.5 collective-permute-done.9
  75.0 1.1 pad_maximum_fusion.1.near_ref
  76.9 4.2 %collective-permute-start.16 = (f32[1,1,64,256]{3,2,0,1:T(8,128)S(1)}, f32[1,1,64,256]{3,2,0,1:T(8,128)S(1)}, u32[]{:S(2)}, u32[]{:S(2)}) collective-permute-start(f32[1,1,64,256]{3,2,0,1:T(8,128)S(1)} %fusion), channel_id=1, source_target_pairs={{0,16},{4,20},{8,24},{12,28},{16,0},{20,4},{24,8},{28,12},{1,17},{... | collective-permute-start | bytes 196616 | tf_op jit(solution)/shard_map/ppermute | solution.py:304
  81.1 4.2 %collective-permute-done.16 = f32[1,1,64,256]{3,2,0,1:T(8,128)S(1)} collective-permute-done((f32[1,1,64,256]{3,2,0,1:T(8,128)S(1)}, f32[1,1,64,256]{3,2,0,1:T(8,128)S(1)}, u32[]{:S(2)}, u32[]{:S(2)}) %collective-permute-start.16) | collective-permute-done | bytes 65568 | tf_op jit(solution)/shard_map/ppermute | solution.py:304
  88.2 1.1 copy-done.8
  89.4 2.8 %shard_map.40 = (bf16[1,256,256]{2,1,0:T(8,128)(2,1)S(1)}, bf16[1,256,256]{2,1,0:T(8,128)(2,1)S(1)}) custom-call(f32[3,256,256]{2,1,0:T(8,128)S(1)} %copy-done.8, f32[1,320,256]{2,1,0:T(8,128)S(1)} %get-tuple-element.54.own_ref, f32[1,320,256]{2,1,0:T(8,128)S(1)} %bitcast.32), custom_call_target="tpu_custom_call" | custom-call | flops 603979776 | bytes 1703936 | tf_op jit(solution)/shard_map/pallas_call | solution.py:290
  93.2 1.6 collective-permute-start.18
  94.7 2.2 collective-permute-done.2.far_ref
  96.9 2.2 shard_map.41
  99.1 2.5 collective-permute-start.4
  101.7 16.2 %collective-permute-done.23.far_ref = f32[256,1024]{1,0:T(8,128)} collective-permute-done((f32[256,1024]{1,0:T(8,128)S(1)}, f32[256,1024]{1,0:T(8,128)}, u32[]{:S(2)}, u32[]{:S(2)}) %collective-permute-start.23) | collective-permute-done | bytes 1048608 | tf_op jit(solution)/shard_map/ppermute | solution.py:304
  117.8 1.9 shard_map.49
  119.7 2.5 collective-permute-start.24
  122.2 3.4 %collective-permute-start.25 = (f32[256,256]{1,0:T(8,128)S(1)}, f32[256,256]{1,0:T(8,128)S(1)}, u32[]{:S(2)}, u32[]{:S(2)}) collective-permute-start(f32[256,256]{1,0:T(8,128)S(1)} %get-tuple-element.85), channel_id=1, source_target_pairs={{0,16},{4,20},{8,24},{12,28},{16,0},{20,4},{24,8},{28,12},{1,17},{... | collective-permute-start | bytes 786440 | tf_op jit(solution)/shard_map/ppermute | solution.py:304
  125.6 8.3 %shard_map.42 = (bf16[2,4,256,256]{3,2,1,0:T(8,128)(2,1)S(1)}, bf16[2,4,256,256]{3,2,1,0:T(8,128)(2,1)S(1)}, bf16[2,4,256,256]{3,2,1,0:T(8,128)(2,1)S(1)}, bf16[2,4,256,256]{3,2,1,0:T(8,128)(2,1)}) custom-call(s32[1]{0:T(128)} %bitcast.1.position_ref, f32[2,4,2,64,256]{4,3,2,1,0:T(8,128)} %pad_maximum_fusion.1.near_ref, ...), custom_call_target="tpu_custom_call" | custom-call | flops 2818572288 | bytes 6291460 | tf_op jit(solution)/shard_map/pallas_call | solution.py:290
  136.9 7.5 %shard_map.43 = (bf16[4,256,256]{2,1,0:T(8,128)(2,1)S(1)}, bf16[4,256,256]{2,1,0:T(8,128)(2,1)S(1)}, bf16[1,4,256,256]{3,2,1,0:T(8,128)(2,1)S(1)}, bf16[1,4,256,256]{3,2,1,0:T(8,128)(2,1)S(1)}) custom-call(s32[1]{0:T(128)} %bitcast.1.position_ref, f32[2,4,4,64,256]{4,3,2,1,0:T(8,128)} %pad_maximum_fusion.near_ref, ...), custom_call_target="tpu_custom_call" | custom-call | flops 3221225472 | bytes 6291460 | tf_op jit(solution)/shard_map/pallas_call | solution.py:290
  144.4 2.1 collective-permute-start.5
  146.5 1.8 collective-permute-start.6
  148.4 6.6 %shard_map.50 = (f32[4,256,256]{2,1,0:T(8,128)}, f32[4,256,256]{2,1,0:T(8,128)}) custom-call(f32[256,256]{1,0:T(8,128)S(1)} %get-tuple-element.83.refs_0_, f32[256,256]{1,0:T(8,128)S(1)} %collective-permute-done.24.refs_1_, f32[256,256]{1,0:T(8,128)S(1)} %collective-permute-done.25.refs_2_, f32[256,256]{1,0:T(8,128)S(1)} %collective-permute-done.26.refs_3_, ...), custom_call_target="tpu_custom_call" | custom-call | flops 2415919104 | bytes 9437184 | tf_op jit(solution)/shard_map/pallas_call | solution.py:290
  155.0 1.4 collective-permute-start.27
  156.5 11.0 %collective-permute-done.5.refs_2_ = f32[256,256]{1,0:T(8,128)S(1)} collective-permute-done((f32[256,256]{1,0:T(8,128)S(1)}, f32[256,256]{1,0:T(8,128)S(1)}, u32[]{:S(2)}, u32[]{:S(2)}) %collective-permute-start.5) | collective-permute-done | bytes 262176 | tf_op jit(solution)/shard_map/ppermute | solution.py:304
  167.5 6.6 %shard_map.44 = (f32[4,256,256]{2,1,0:T(8,128)}, f32[4,256,256]{2,1,0:T(8,128)}) custom-call(f32[256,256]{1,0:T(8,128)S(1)} %get-tuple-element.57.refs_0_, f32[256,256]{1,0:T(8,128)S(1)} %collective-permute-done.4.refs_1_, f32[256,256]{1,0:T(8,128)S(1)} %collective-permute-done.5.refs_2_, f32[256,256]{1,0:T(8,128)S(1)} %collective-permute-done.6.refs_3_, ...), custom_call_target="tpu_custom_call" | custom-call | flops 2415919104 | bytes 9437184 | tf_op jit(solution)/shard_map/pallas_call | solution.py:290
  174.1 12.0 %collective-permute-start.15 = (f32[4,256,256]{2,1,0:T(8,128)}, f32[4,256,256]{2,1,0:T(8,128)S(1)}, u32[]{:S(2)}, u32[]{:S(2)}) collective-permute-start(f32[4,256,256]{2,1,0:T(8,128)} %get-tuple-element.70.refs_1_), channel_id=1, source_target_pairs={{0,4},{4,0},{8,12},{12,8},{16,20},{20,16},{24,28},{28,24},{1,5},{5... | collective-permute-start | bytes 3145736 | tf_op jit(solution)/shard_map/ppermute | solution.py:304
  186.2 6.4 %shard_map.45 = (bf16[1,4,256,256]{3,2,1,0:T(8,128)(2,1)S(1)}, bf16[1,4,256,256]{3,2,1,0:T(8,128)(2,1)S(1)}) custom-call(s32[1]{0:T(128)} %bitcast.1.position_ref, f32[2,4,4,64,256]{4,3,2,1,0:T(8,128)} %pad_maximum_fusion.near_ref, f32[2,4,4,64,256]{4,3,2,1,0:T(8,128)} %collective-permute-done.14.far_ref, ...), custom_call_target="tpu_custom_call" | custom-call | flops 2013265920 | bytes 6291460 | tf_op jit(solution)/shard_map/pallas_call | solution.py:290
  192.6 8.8 %shard_map.46 = (bf16[2,4,256,256]{3,2,1,0:T(8,128)(2,1)S(1)}, bf16[2,4,256,256]{3,2,1,0:T(8,128)(2,1)S(1)}, bf16[2,4,256,256]{3,2,1,0:T(8,128)(2,1)S(1)}, bf16[2,4,256,256]{3,2,1,0:T(8,128)(2,1)}) custom-call(s32[1]{0:T(128)} %bitcast.1.position_ref, f32[2,4,4,64,256]{4,3,2,1,0:T(8,128)} %pad_maximum_fusion.near_ref, ...), custom_call_target="tpu_custom_call" | custom-call | flops 2818572288 | bytes 8388612 | tf_op jit(solution)/shard_map/pallas_call | solution.py:290
  205.4 5.5 %shard_map.51 = (f32[256,256]{1,0:T(8,128)S(1)}, f32[256,256]{1,0:T(8,128)S(1)}, f32[256,256]{1,0:T(8,128)S(1)}, f32[256,256]{1,0:T(8,128)S(1)}) custom-call(f32[4,256,256]{2,1,0:T(8,128)S(1)} %copy-done.3, f32[4,256,256]{2,1,0:T(8,128)} %get-tuple-element.88.refs_1_, f32[4,256,256]{2,1,0:T(8,128)} %copy-done.13, ...), custom_call_target="tpu_custom_call" | custom-call | flops 2013265920 | bytes 9437184 | tf_op jit(solution)/shard_map/pallas_call | solution.py:290
  210.9 4.3 %collective-permute-start.28 = (f32[256,256]{1,0:T(8,128)S(1)}, f32[256,256]{1,0:T(8,128)S(1)}, u32[]{:S(2)}, u32[]{:S(2)}) collective-permute-start(f32[256,256]{1,0:T(8,128)S(1)} %get-tuple-element.90), channel_id=1, source_target_pairs={{0,8},{4,12},{8,0},{12,4},{16,24},{20,28},{24,16},{28,20},{1,9},{5... | collective-permute-start | bytes 786440 | tf_op jit(solution)/shard_map/ppermute | solution.py:304
  215.2 2.4 collective-permute-start.30
  218.7 5.4 %shard_map.47 = (f32[256,256]{1,0:T(8,128)S(1)}, f32[256,256]{1,0:T(8,128)S(1)}, f32[256,256]{1,0:T(8,128)S(1)}, f32[256,256]{1,0:T(8,128)S(1)}) custom-call(f32[4,256,256]{2,1,0:T(8,128)S(1)} %copy-done.4, f32[4,256,256]{2,1,0:T(8,128)} %get-tuple-element.70.refs_1_, f32[4,256,256]{2,1,0:T(8,128)} %copy-done.14, ...), custom_call_target="tpu_custom_call" | custom-call | flops 2013265920 | bytes 9437184 | tf_op jit(solution)/shard_map/pallas_call | solution.py:290
  224.0 1.1 collective-permute-start.20
  226.1 2.4 collective-permute-start.22
  228.5 8.2 %collective-permute-done.29.refs_6_ = f32[256,256]{1,0:T(8,128)S(1)} collective-permute-done((f32[256,256]{1,0:T(8,128)S(1)}, f32[256,256]{1,0:T(8,128)S(1)}, u32[]{:S(2)}, u32[]{:S(2)}) %collective-permute-start.29) | collective-permute-done | bytes 262176 | tf_op jit(solution)/shard_map/ppermute | solution.py:304
  236.7 2.1 collective-permute-done.20.refs_1_
  238.9 19.8 %collective-permute-done.21.refs_2_ = f32[256,256]{1,0:T(8,128)S(1)} collective-permute-done((f32[256,256]{1,0:T(8,128)S(1)}, f32[256,256]{1,0:T(8,128)S(1)}, u32[]{:S(2)}, u32[]{:S(2)}) %collective-permute-start.21) | collective-permute-done | bytes 262176 | tf_op jit(solution)/shard_map/ppermute | solution.py:304
  258.7 1.5 shard_map.52
  (84 shorter events, 20.8 us)
Async XLA Ops:
  0.9 31.7 %copy-start.15 = (f32[2,3,256,64]{2,3,1,0:T(8,128)S(1)}, f32[2,3,256,64]{2,3,1,0:T(8,128)}, u32[]{:S(2)}) copy-start(f32[2,3,256,64]{2,3,1,0:T(8,128)} %param.5) | copy-start | bytes 1179652
  1.9 16.0 %collective-permute-start.11 = (f32[1,4,64,256]{3,2,1,0:T(8,128)S(1)}, f32[1,4,64,256]{3,2,1,0:T(8,128)S(1)}, u32[]{:S(2)}, u32[]{:S(2)}) collective-permute-start(f32[1,4,64,256]{3,2,1,0:T(8,128)S(1)} %maximum_bitcast_fusion.2), channel_id=1, source_target_pairs={{0,16},{4,20},{8,24},{12,28},{16,0},{20,4},{24,8},{28,12},{1,17},{... | collective-permute-start | bytes 786440 | tf_op jit(solution)/shard_map/ppermute | solution.py:304
  18.0 13.2 %collective-permute-start.12 = (f32[2,4,64,256]{3,2,1,0:T(8,128)S(1)}, f32[2,4,64,256]{3,2,1,0:T(8,128)S(1)}, u32[]{:S(2)}, u32[]{:S(2)}) collective-permute-start(f32[2,4,64,256]{3,2,1,0:T(8,128)S(1)} %pad_maximum_fusion.2), channel_id=1, source_target_pairs={{0,8},{4,12},{8,0},{12,4},{16,24},{20,28},{24,16},{28,20},{1,9},{5... | collective-permute-start | bytes 1572872 | tf_op jit(solution)/shard_map/ppermute | solution.py:304
  31.3 27.8 %collective-permute-start.13 = (f32[1,4,4,64,256]{4,3,2,1,0:T(8,128)S(1)}, f32[1,4,4,64,256]{4,3,2,1,0:T(8,128)S(1)}, u32[]{:S(2)}, u32[]{:S(2)}) collective-permute-start(f32[1,4,4,64,256]{4,3,2,1,0:T(8,128)S(1)} %maximum_bitcast_fusion), channel_id=1, source_target_pairs={{0,2},{1,3},{2,0},{3,1},{4,6},{5,7},{6,4},{7,5},{8,10},{9,11},{10,... | collective-permute-start | bytes 3145736 | tf_op jit(solution)/shard_map/ppermute | solution.py:304
  32.6 9.1 %collective-permute-start.7 = (f32[1,2,64,256]{3,2,1,0:T(8,128)S(1)}, f32[1,2,64,256]{3,2,1,0:T(8,128)S(1)}, u32[]{:S(2)}, u32[]{:S(2)}) collective-permute-start(f32[1,2,64,256]{3,2,1,0:T(8,128)S(1)} %slice.43), channel_id=1, source_target_pairs={{0,16},{4,20},{8,24},{12,28},{16,0},{20,4},{24,8},{28,12},{1,17},{... | collective-permute-start | bytes 393224 | tf_op jit(solution)/shard_map/ppermute | solution.py:304
  36.0 22.9 %collective-permute-start = (f32[1,1,3,64,256]{4,3,2,1,0:T(8,128)S(1)}, f32[1,1,3,64,256]{4,3,2,1,0:T(8,128)S(1)}, u32[]{:S(2)}, u32[]{:S(2)}) collective-permute-start(f32[1,1,3,64,256]{4,3,2,1,0:T(8,128)S(1)} %maximum_bitcast_fusion.4), channel_id=1, source_target_pairs={{0,2},{1,3},{2,0},{3,1},{4,6},{5,7},{6,4},{7,5},{8,10},{9,11},{10,... | collective-permute-start | bytes 589832 | tf_op jit(solution)/shard_map/ppermute | solution.py:304
  41.7 19.4 %collective-permute-start.8 = (f32[2,2,64,256]{3,2,1,0:T(8,128)S(1)}, f32[2,2,64,256]{3,2,1,0:T(8,128)S(1)}, u32[]{:S(2)}, u32[]{:S(2)}) collective-permute-start(f32[2,2,64,256]{3,2,1,0:T(8,128)S(1)} %pad_maximum_fusion.5), channel_id=1, source_target_pairs={{0,8},{4,12},{8,0},{12,4},{16,24},{20,28},{24,16},{28,20},{1,9},{5... | collective-permute-start | bytes 786440 | tf_op jit(solution)/shard_map/ppermute | solution.py:304
  59.0 3.5 %copy-start.12 = (f32[256,2048]{1,0:T(8,128)S(1)}, f32[256,2048]{1,0:T(8,128)}, u32[]{:S(2)}) copy-start(f32[256,2048]{1,0:T(8,128)} %param.3) | copy-start | bytes 6291460
  59.0 3.7 %collective-permute-start.1 = (f32[2,1,3,64,256]{4,3,2,1,0:T(8,128)S(1)}, f32[2,1,3,64,256]{4,3,2,1,0:T(8,128)S(1)}, u32[]{:S(2)}, u32[]{:S(2)}) collective-permute-start(f32[2,1,3,64,256]{4,3,2,1,0:T(8,128)S(1)} %pad_maximum_fusion.4.near_ref), channel_id=1, source_target_pairs={{0,1},{1,0},{2,3},{3,2},{4,5},{5,4},{6,7},{7,6},{8,9},{9,8},{10,11... | collective-permute-start | bytes 1179656 | tf_op jit(solution)/shard_map/ppermute | solution.py:304
  60.6 76.3 %collective-permute-start.14 = (f32[2,4,4,64,256]{4,3,2,1,0:T(8,128)}, f32[2,4,4,64,256]{4,3,2,1,0:T(8,128)}, u32[]{:S(2)}, u32[]{:S(2)}) collective-permute-start(f32[2,4,4,64,256]{4,3,2,1,0:T(8,128)} %pad_maximum_fusion.near_ref), channel_id=1, source_target_pairs={{0,1},{1,0},{2,3},{3,2},{4,5},{5,4},{6,7},{7,6},{8,9},{9,8},{10,11... | collective-permute-start | bytes 6291464 | tf_op jit(solution)/shard_map/ppermute | solution.py:304
  61.1 13.9 %collective-permute-start.9 = (f32[1,4,2,64,256]{4,3,2,1,0:T(8,128)S(1)}, f32[1,4,2,64,256]{4,3,2,1,0:T(8,128)S(1)}, u32[]{:S(2)}, u32[]{:S(2)}) collective-permute-start(f32[1,4,2,64,256]{4,3,2,1,0:T(8,128)S(1)} %maximum_bitcast_fusion.1), channel_id=1, source_target_pairs={{0,2},{1,3},{2,0},{3,1},{4,6},{5,7},{6,4},{7,5},{8,10},{9,11},{10,... | collective-permute-start | bytes 1572872 | tf_op jit(solution)/shard_map/ppermute | solution.py:304
  63.2 5.3 %copy-start.7 = (f32[3,256,256]{2,1,0:T(8,128)}, f32[3,256,256]{2,1,0:T(8,128)S(1)}, u32[]{:S(2)}) copy-start(f32[3,256,256]{2,1,0:T(8,128)S(1)} %get-tuple-element.49.vectors_ref) | copy-start | bytes 2359300
  63.2 12.9 %collective-permute-start.3 = (f32[320,256]{1,0:T(8,128)S(1)}, f32[320,256]{1,0:T(8,128)S(1)}, u32[]{:S(2)}, u32[]{:S(2)}) collective-permute-start(f32[320,256]{1,0:T(8,128)S(1)} %bitcast.30), channel_id=1, source_target_pairs={{0,4},{4,0},{8,12},{12,8},{16,20},{20,16},{24,28},{28,24},{1,5},{5... | collective-permute-start | bytes 983048 | tf_op jit(solution)/shard_map/ppermute | solution.py:304
  70.5 26.4 %collective-permute-start.2 = (f32[256,1024]{1,0:T(8,128)}, f32[256,1024]{1,0:T(8,128)}, u32[]{:S(2)}, u32[]{:S(2)}) collective-permute-start(f32[256,1024]{1,0:T(8,128)} %get-tuple-element.53.own_ref), channel_id=1, source_target_pairs={{0,4},{4,0},{8,12},{12,8},{16,20},{20,16},{24,28},{28,24},{1,5},{5... | collective-permute-start | bytes 3145736 | tf_op jit(solution)/shard_map/ppermute | solution.py:304
  72.0 45.8 %collective-permute-start.23 = (f32[256,1024]{1,0:T(8,128)S(1)}, f32[256,1024]{1,0:T(8,128)}, u32[]{:S(2)}, u32[]{:S(2)}) collective-permute-start(f32[256,1024]{1,0:T(8,128)S(1)} %get-tuple-element.82.own_ref), channel_id=1, source_target_pairs={{0,4},{4,0},{8,12},{12,8},{16,20},{20,16},{24,28},{28,24},{1,5},{5... | collective-permute-start | bytes 3145736 | tf_op jit(solution)/shard_map/ppermute | solution.py:304
  76.1 46.1 %collective-permute-start.10 = (f32[2,4,2,64,256]{4,3,2,1,0:T(8,128)}, f32[2,4,2,64,256]{4,3,2,1,0:T(8,128)}, u32[]{:S(2)}, u32[]{:S(2)}) collective-permute-start(f32[2,4,2,64,256]{4,3,2,1,0:T(8,128)} %pad_maximum_fusion.1.near_ref), channel_id=1, source_target_pairs={{0,1},{1,0},{2,3},{3,2},{4,5},{5,4},{6,7},{7,6},{8,9},{9,8},{10,11... | collective-permute-start | bytes 3145736 | tf_op jit(solution)/shard_map/ppermute | solution.py:304
  76.1 0.8 copy-start.5
  76.9 8.4 %collective-permute-start.16 = (f32[1,1,64,256]{3,2,0,1:T(8,128)S(1)}, f32[1,1,64,256]{3,2,0,1:T(8,128)S(1)}, u32[]{:S(2)}, u32[]{:S(2)}) collective-permute-start(f32[1,1,64,256]{3,2,0,1:T(8,128)S(1)} %fusion), channel_id=1, source_target_pairs={{0,16},{4,20},{8,24},{12,28},{16,0},{20,4},{24,8},{28,12},{1,17},{... | collective-permute-start | bytes 196616 | tf_op jit(solution)/shard_map/ppermute | solution.py:304
  86.6 5.6 %collective-permute-start.17 = (f32[2,1,64,256]{3,2,0,1:T(8,128)}, f32[2,1,64,256]{3,2,0,1:T(8,128)}, u32[]{:S(2)}, u32[]{:S(2)}) collective-permute-start(f32[2,1,64,256]{3,2,0,1:T(8,128)} %pad_maximum_fusion.6), channel_id=1, source_target_pairs={{0,8},{4,12},{8,0},{12,4},{16,24},{20,28},{24,16},{28,20},{1,9},{5... | collective-permute-start | bytes 393224 | tf_op jit(solution)/shard_map/ppermute | solution.py:304
  87.3 1.0 copy-start.6
  88.2 1.1 copy-start.8
  89.4 2.9 %copy-start.17 = (f32[1,1,64,256]{3,2,0,1:T(8,128)S(1)}, f32[1,1,64,256]{3,2,0,1:T(8,128)}, u32[]{:S(2)}) copy-start(f32[1,1,64,256]{3,2,0,1:T(8,128)} %copy-done.16) | copy-start | bytes 196612
  93.2 63.2 %collective-permute-start.18 = (f32[1,4,1,64,256]{4,3,2,1,0:T(8,128)S(1)}, f32[1,4,1,64,256]{4,3,2,1,0:T(8,128)S(1)}, u32[]{:S(2)}, u32[]{:S(2)}) collective-permute-start(f32[1,4,1,64,256]{4,3,2,1,0:T(8,128)S(1)} %maximum_bitcast_fusion.3), channel_id=1, source_target_pairs={{0,2},{1,3},{2,0},{3,1},{4,6},{5,7},{6,4},{7,5},{8,10},{9,11},{10,... | collective-permute-start | bytes 786440 | tf_op jit(solution)/shard_map/ppermute | solution.py:304
  99.1 57.4 %collective-permute-start.4 = (f32[256,256]{1,0:T(8,128)S(1)}, f32[256,256]{1,0:T(8,128)S(1)}, u32[]{:S(2)}, u32[]{:S(2)}) collective-permute-start(f32[256,256]{1,0:T(8,128)S(1)} %get-tuple-element.58), channel_id=1, source_target_pairs={{0,8},{4,12},{8,0},{12,4},{16,24},{20,28},{24,16},{28,20},{1,9},{5... | collective-permute-start | bytes 786440 | tf_op jit(solution)/shard_map/ppermute | solution.py:304
  119.7 24.7 %collective-permute-start.24 = (f32[256,256]{1,0:T(8,128)S(1)}, f32[256,256]{1,0:T(8,128)S(1)}, u32[]{:S(2)}, u32[]{:S(2)}) collective-permute-start(f32[256,256]{1,0:T(8,128)S(1)} %get-tuple-element.84), channel_id=1, source_target_pairs={{0,8},{4,12},{8,0},{12,4},{16,24},{20,28},{24,16},{28,20},{1,9},{5... | collective-permute-start | bytes 786440 | tf_op jit(solution)/shard_map/ppermute | solution.py:304
  122.2 24.3 %collective-permute-start.25 = (f32[256,256]{1,0:T(8,128)S(1)}, f32[256,256]{1,0:T(8,128)S(1)}, u32[]{:S(2)}, u32[]{:S(2)}) collective-permute-start(f32[256,256]{1,0:T(8,128)S(1)} %get-tuple-element.85), channel_id=1, source_target_pairs={{0,16},{4,20},{8,24},{12,28},{16,0},{20,4},{24,8},{28,12},{1,17},{... | collective-permute-start | bytes 786440 | tf_op jit(solution)/shard_map/ppermute | solution.py:304
  133.9 1.1 copy-start.9
  134.9 1.0 copy-start.10
  135.9 1.0 copy-start.11
  136.9 11.5 %collective-permute-start.26 = (f32[256,256]{1,0:T(8,128)S(1)}, f32[256,256]{1,0:T(8,128)S(1)}, u32[]{:S(2)}, u32[]{:S(2)}) collective-permute-start(f32[256,256]{1,0:T(8,128)S(1)} %get-tuple-element.86), channel_id=1, source_target_pairs={{0,24},{4,28},{8,16},{12,20},{16,8},{20,12},{24,0},{28,4},{1,25},{... | collective-permute-start | bytes 786440 | tf_op jit(solution)/shard_map/ppermute | solution.py:304
  144.4 23.1 %collective-permute-start.5 = (f32[256,256]{1,0:T(8,128)S(1)}, f32[256,256]{1,0:T(8,128)S(1)}, u32[]{:S(2)}, u32[]{:S(2)}) collective-permute-start(f32[256,256]{1,0:T(8,128)S(1)} %get-tuple-element.59), channel_id=1, source_target_pairs={{0,16},{4,20},{8,24},{12,28},{16,0},{20,4},{24,8},{28,12},{1,17},{... | collective-permute-start | bytes 786440 | tf_op jit(solution)/shard_map/ppermute | solution.py:304
  146.5 21.0 %collective-permute-start.6 = (f32[256,256]{1,0:T(8,128)S(1)}, f32[256,256]{1,0:T(8,128)S(1)}, u32[]{:S(2)}, u32[]{:S(2)}) collective-permute-start(f32[256,256]{1,0:T(8,128)S(1)} %get-tuple-element.60), channel_id=1, source_target_pairs={{0,24},{4,28},{8,16},{12,20},{16,8},{20,12},{24,0},{28,4},{1,25},{... | collective-permute-start | bytes 786440 | tf_op jit(solution)/shard_map/ppermute | solution.py:304
  155.0 49.4 %collective-permute-start.27 = (f32[4,256,256]{2,1,0:T(8,128)}, f32[4,256,256]{2,1,0:T(8,128)S(1)}, u32[]{:S(2)}, u32[]{:S(2)}) collective-permute-start(f32[4,256,256]{2,1,0:T(8,128)} %get-tuple-element.88.refs_1_), channel_id=1, source_target_pairs={{0,4},{4,0},{8,12},{12,8},{16,20},{20,16},{24,28},{28,24},{1,5},{5... | collective-permute-start | bytes 3145736 | tf_op jit(solution)/shard_map/ppermute | solution.py:304
  156.4 29.7 %collective-permute-start.19 = (f32[2,4,1,64,256]{4,3,2,1,0:T(8,128)S(1)}, f32[2,4,1,64,256]{4,3,2,1,0:T(8,128)S(1)}, u32[]{:S(2)}, u32[]{:S(2)}) collective-permute-start(f32[2,4,1,64,256]{4,3,2,1,0:T(8,128)S(1)} %pad_maximum_fusion.3.gram_near), channel_id=1, source_target_pairs={{0,1},{1,0},{2,3},{3,2},{4,5},{5,4},{6,7},{7,6},{8,9},{9,8},{10,11... | collective-permute-start | bytes 1572872 | tf_op jit(solution)/shard_map/ppermute | solution.py:304
  174.1 43.6 %collective-permute-start.15 = (f32[4,256,256]{2,1,0:T(8,128)}, f32[4,256,256]{2,1,0:T(8,128)S(1)}, u32[]{:S(2)}, u32[]{:S(2)}) collective-permute-start(f32[4,256,256]{2,1,0:T(8,128)} %get-tuple-element.70.refs_1_), channel_id=1, source_target_pairs={{0,4},{4,0},{8,12},{12,8},{16,20},{20,16},{24,28},{28,24},{1,5},{5... | collective-permute-start | bytes 3145736 | tf_op jit(solution)/shard_map/ppermute | solution.py:304
  192.6 12.8 %copy-start.3 = (f32[4,256,256]{2,1,0:T(8,128)S(1)}, f32[4,256,256]{2,1,0:T(8,128)}, u32[]{:S(2)}) copy-start(f32[4,256,256]{2,1,0:T(8,128)} %get-tuple-element.87.refs_0_) | copy-start | bytes 3145732
  201.4 1.0 copy-start
  202.4 1.0 copy-start.1
  203.4 1.1 copy-start.2
  204.4 1.0 copy-start.13
  205.4 13.3 %copy-start.4 = (f32[4,256,256]{2,1,0:T(8,128)S(1)}, f32[4,256,256]{2,1,0:T(8,128)}, u32[]{:S(2)}) copy-start(f32[4,256,256]{2,1,0:T(8,128)} %get-tuple-element.69.refs_0_) | copy-start | bytes 3145732
  210.9 15.2 %collective-permute-start.28 = (f32[256,256]{1,0:T(8,128)S(1)}, f32[256,256]{1,0:T(8,128)S(1)}, u32[]{:S(2)}, u32[]{:S(2)}) collective-permute-start(f32[256,256]{1,0:T(8,128)S(1)} %get-tuple-element.90), channel_id=1, source_target_pairs={{0,8},{4,12},{8,0},{12,4},{16,24},{20,28},{24,16},{28,20},{1,9},{5... | collective-permute-start | bytes 786440 | tf_op jit(solution)/shard_map/ppermute | solution.py:304
  215.2 21.5 %collective-permute-start.29 = (f32[256,256]{1,0:T(8,128)S(1)}, f32[256,256]{1,0:T(8,128)S(1)}, u32[]{:S(2)}, u32[]{:S(2)}) collective-permute-start(f32[256,256]{1,0:T(8,128)S(1)} %get-tuple-element.91), channel_id=1, source_target_pairs={{0,16},{4,20},{8,24},{12,28},{16,0},{20,4},{24,8},{28,12},{1,17},{... | collective-permute-start | bytes 786440 | tf_op jit(solution)/shard_map/ppermute | solution.py:304
  215.2 21.5 %collective-permute-start.30 = (f32[256,256]{1,0:T(8,128)S(1)}, f32[256,256]{1,0:T(8,128)S(1)}, u32[]{:S(2)}, u32[]{:S(2)}) collective-permute-start(f32[256,256]{1,0:T(8,128)S(1)} %get-tuple-element.92), channel_id=1, source_target_pairs={{0,24},{4,28},{8,16},{12,20},{16,8},{20,12},{24,0},{28,4},{1,25},{... | collective-permute-start | bytes 786440 | tf_op jit(solution)/shard_map/ppermute | solution.py:304
  217.7 1.0 copy-start.14
  224.0 14.8 %collective-permute-start.20 = (f32[256,256]{1,0:T(8,128)S(1)}, f32[256,256]{1,0:T(8,128)S(1)}, u32[]{:S(2)}, u32[]{:S(2)}) collective-permute-start(f32[256,256]{1,0:T(8,128)S(1)} %get-tuple-element.78), channel_id=1, source_target_pairs={{0,8},{4,12},{8,0},{12,4},{16,24},{20,28},{24,16},{28,20},{1,9},{5... | collective-permute-start | bytes 786440 | tf_op jit(solution)/shard_map/ppermute | solution.py:304
  225.2 33.5 %collective-permute-start.21 = (f32[256,256]{1,0:T(8,128)S(1)}, f32[256,256]{1,0:T(8,128)S(1)}, u32[]{:S(2)}, u32[]{:S(2)}) collective-permute-start(f32[256,256]{1,0:T(8,128)S(1)} %get-tuple-element.79), channel_id=1, source_target_pairs={{0,16},{4,20},{8,24},{12,28},{16,0},{20,4},{24,8},{28,12},{1,17},{... | collective-permute-start | bytes 786440 | tf_op jit(solution)/shard_map/ppermute | solution.py:304
  226.1 32.6 %collective-permute-start.22 = (f32[256,256]{1,0:T(8,128)S(1)}, f32[256,256]{1,0:T(8,128)S(1)}, u32[]{:S(2)}, u32[]{:S(2)}) collective-permute-start(f32[256,256]{1,0:T(8,128)S(1)} %get-tuple-element.80), channel_id=1, source_target_pairs={{0,24},{4,28},{8,16},{12,20},{16,8},{20,12},{24,0},{28,4},{1,25},{... | collective-permute-start | bytes 786440 | tf_op jit(solution)/shard_map/ppermute | solution.py:304
  (1 other events, 0.6 us)
